TPU v7x, 32 devices: a whole 2x2x4 slice. The times are simulated.
32 devices in a mesh: groups: 2 (over y), depth: 4 (over z), dp: 2 (over x), sub: 2 (over core).
Axes of the slice: x: 2, y: 2, z: 4, core: 2. Of those that a mesh axis runs over, the one named last changes fastest.
Arguments:
- objects: float32 [16, 2, 512, 512], P(('groups', 'depth'), None, 'sub'), parts along dimension 0, may hold values from -1.1 to 1.1, as said below
- probe_wave: float32 [2, 256, 256], replicated, may hold values from -6 to 6
- offsets: int32 [32, 2], P(('groups', 'dp', 'sub')), parts along dimension 0, may hold values from 0 to 256
- counts: int32 [32, 256, 256], P(('groups', 'dp', 'sub')), parts along dimension 0, may hold values from 0 to 7
Outputs:
- object_grad: float32 [16, 2, 512, 512], P(('groups', 'depth'), None, ('dp', 'sub')), parts along dimension 0
There are 2 independent parts, one for each index of `groups`. A program takes and returns all parts, laid end to end along the dimension named above; an argument that names none is the same for every part. Nothing has to cross between parts.
Inputs may be any that keep to these rules, and one draw needn't show every extreme that they name: The pair objects[k,0,r,c], objects[k,1,r,c] has magnitude between 0.8 and 1.1.
All inputs are finite; a program needn't handle non-finite values.
Results may differ from a plain program's by a relative error of at most 0.0003.
Values sent between devices are 32-bit elements; how exact they have to be, the bound alone decides.
A program may use at most 128 MiB of HBM per device.

v0:
```python
import functools

import jax
import jax.numpy as jnp
import numpy as np
from jax import lax
from jax.experimental import pallas as pl
from jax.experimental.pallas import tpu as pltpu
from jax.sharding import PartitionSpec as P

KAPPA = 40.0
MESH = pl.DeviceIdType.MESH


def split_tables(matrix):
    real, imag = matrix.real, matrix.imag
    right = np.block([[real, imag], [-imag, real]]).astype(np.float32)
    tables = []
    for block in (right, right.T):
        high = block.astype(jnp.bfloat16)
        low = (block - high.astype(np.float32)).astype(jnp.bfloat16)
        tables += [high, low]
    return np.stack(tables)


def constants(size):
    index = np.arange(size)
    fourier = np.exp(-2j * np.pi * (index[:, None] * index[None, :] % size) / size)
    frequency = np.where(index < size // 2, index, index - size) / size
    ramp = np.exp(-1j * KAPPA * frequency**2)
    circulant = np.conj(fourier) @ (ramp[:, None] * fourier) / size
    circulant = 0.5 * (circulant + circulant.T)
    return split_tables(circulant), split_tables(fourier / np.sqrt(size))


def two_terms(value):
    high = value.astype(jnp.bfloat16)
    low = (value - high.astype(jnp.float32)).astype(jnp.bfloat16)
    return high, low


def dot(left, right):
    return jnp.dot(left, right, preferred_element_type=jnp.float32)


def rows_up(value, shift):
    tiles = value.reshape(value.shape[0] // 8, 8, value.shape[1])
    turned = pltpu.roll(tiles, lax.rem(8 - shift, 8), 1)
    place = lax.broadcasted_iota(jnp.int32, turned[1:].shape, 1)
    moved = jnp.where(place < 8 - shift, turned[:-1], turned[1:])
    return moved.reshape(value.shape[0] - 8, value.shape[1])


def both_sides(real, imag, table):
    size = real.shape[0]
    high, low = two_terms(jnp.concatenate([real, imag], axis=1))
    rows = dot(high, table[0]) + dot(low, table[0]) + dot(high, table[1])
    high, low = two_terms(jnp.concatenate([rows[:, :size], rows[:, size:]], axis=0))
    both = dot(table[2], high) + dot(table[2], low) + dot(table[3], high)
    return both[:size], both[size:]


def greet(neighbours):
    barrier = pltpu.get_barrier_semaphore()
    for axis, index in neighbours:
        pl.semaphore_signal(barrier, inc=1, device_id={axis: index}, device_id_type=MESH)
    pl.semaphore_wait(barrier, len(neighbours))


def others(axis, count):
    me = lax.axis_index(axis)
    return [(axis, lax.rem(me + shift, count)) for shift in range(1, count)]


def gather_kernel(sub_n, objects, full, send, recv, own_sem):
    sub = lax.axis_index("sub")
    layers, _, half, _ = objects.shape
    greet(others("sub", sub_n))
    mine = pl.ds(pl.multiple_of(sub * half, half), half)
    copies = []
    for shift in range(1, sub_n):
        copy = pltpu.make_async_remote_copy(
            src_ref=objects,
            dst_ref=full.at[:, :, mine],
            send_sem=send.at[shift],
            recv_sem=recv.at[shift],
            device_id={"sub": lax.rem(sub + shift, sub_n)},
            device_id_type=MESH,
        )
        copy.start()
        copies.append(copy)
    own = pltpu.make_async_copy(objects, full.at[:, :, mine], own_sem)
    own.start()
    own.wait()
    for copy in copies:
        copy.wait()


def window_kernel(offsets, full, win):
    positions, layers, _, size, _ = win.shape
    width = full.shape[3]

    @pl.loop(0, positions)
    def _(item):
        row, column = offsets[item, 0], offsets[item, 1]
        row_rest = lax.rem(row, 8)
        row_tile = pl.multiple_of(row - row_rest, 8)
        turn = lax.rem(width - column, width)
        for layer in range(layers):
            for part in range(2):
                strip = full[layer, part, pl.ds(row_tile, size), :]
                last = jnp.minimum(row_tile + size, full.shape[2] - 8)
                tail = full[layer, part, pl.ds(pl.multiple_of(last, 8), 8), :]
                strip = pltpu.roll(jnp.concatenate([strip, tail], axis=0), turn, 1)[:, :size]
                win[item, layer, part] = rows_up(strip, row_rest)


def scatter_kernel(offsets, delta, grad):
    positions, layers, _, size, _ = delta.shape
    width = grad.shape[3]
    grad[...] = jnp.zeros_like(grad)

    @pl.loop(0, positions)
    def _(item):
        row, column = offsets[item, 0], offsets[item, 1]
        row_rest = lax.rem(row, 8)
        row_tile = pl.multiple_of(row - row_rest, 8)
        ends = jnp.zeros((8, size), jnp.float32)
        side_by = jnp.zeros((size + 8, width - size), jnp.float32)
        for layer in range(layers):
            for part in range(2):
                tall = jnp.concatenate([ends, delta[item, layer, part], ends], axis=0)
                wide = jnp.concatenate([rows_up(tall, 8 - row_rest), side_by], axis=1)
                grad[layer, part, pl.ds(row_tile, size + 8), :] += pltpu.roll(wide, column, 1)


def sum_kernel(dp_n, sub_n, grad, out, rsub, acc, rdp, s_send, s_recv, d_send, d_recv):
    dp, sub = lax.axis_index("dp"), lax.axis_index("sub")
    layers, _, rows, _ = out.shape
    greet(others("sub", sub_n) + others("dp", dp_n))
    sub_copies = []
    for layer in range(layers):
        group = []
        for shift in range(1, sub_n):
            other = lax.rem(sub + shift, sub_n)
            for chip in range(dp_n):
                start = pl.multiple_of((chip * sub_n + other) * rows, rows)
                copy = pltpu.make_async_remote_copy(
                    src_ref=grad.at[layer, :, pl.ds(start, rows)],
                    dst_ref=rsub.at[layer, shift, chip],
                    send_sem=s_send.at[layer, shift, chip],
                    recv_sem=s_recv.at[layer, shift, chip],
                    device_id={"sub": other},
                    device_id_type=MESH,
                )
                copy.start()
                group.append(copy)
        sub_copies.append(group)
    dp_copies = []
    for layer, group in enumerate(sub_copies):
        for copy in group:
            copy.wait()
        for chip in range(dp_n):
            start = pl.multiple_of((chip * sub_n + sub) * rows, rows)
            total = grad[layer, :, pl.ds(start, rows), :]
            for shift in range(1, sub_n):
                total = total + rsub[layer, shift, chip]
            acc[layer, chip] = total
        group = []
        for shift in range(1, dp_n):
            other = lax.rem(dp + shift, dp_n)
            copy = pltpu.make_async_remote_copy(
                src_ref=acc.at[layer, other],
                dst_ref=rdp.at[layer, shift],
                send_sem=d_send.at[layer, shift],
                recv_sem=d_recv.at[layer, shift],
                device_id={"dp": other},
                device_id_type=MESH,
            )
            copy.start()
            group.append(copy)
        dp_copies.append(group)
    for layer, group in enumerate(dp_copies):
        for copy in group:
            copy.wait()
        total = acc[layer, dp]
        for shift in range(1, dp_n):
            total = total + rdp[layer, shift]
        out[layer] = total


def wave_kernel(
    depth_n, win, probe, counts, prop_table, far_table, delta,
    fin, mid, fout, bin_, bout, f_send, f_recv, b_send, b_recv,
):
    depth = lax.axis_index("depth")
    positions, layers, _, size, _ = win.shape
    is_first, is_last = depth == 0, depth == depth_n - 1
    following = lax.rem(depth + 1, depth_n)
    previous = lax.rem(depth + depth_n - 1, depth_n)
    greet([("depth", following), ("depth", previous)])

    def forward_copy(item):
        return pltpu.make_async_remote_copy(
            src_ref=fout.at[item],
            dst_ref=fin.at[item],
            send_sem=f_send.at[item],
            recv_sem=f_recv.at[item],
            device_id={"depth": following},
            device_id_type=MESH,
        )

    def backward_copy(item):
        return pltpu.make_async_remote_copy(
            src_ref=bout.at[item],
            dst_ref=bin_.at[item],
            send_sem=b_send.at[item],
            recv_sem=b_recv.at[item],
            device_id={"depth": previous},
            device_id_type=MESH,
        )

    def forward(item):
        @pl.when(is_first)
        def _():
            fin[item] = probe[...]

        @pl.when(jnp.logical_not(is_first))
        def _():
            forward_copy(item).wait_recv()

        real, imag = fin[item, 0], fin[item, 1]
        for layer in range(layers):
            if layer > 0:
                mid[item, layer - 1, 0] = real
                mid[item, layer - 1, 1] = imag
            obj_re, obj_im = win[item, layer, 0], win[item, layer, 1]
            real, imag = both_sides(
                real * obj_re - imag * obj_im, real * obj_im + imag * obj_re, prop_table
            )
        fout[item, 0] = real
        fout[item, 1] = imag

        @pl.when(jnp.logical_not(is_last))
        def _():
            forward_copy(item).start()

        @pl.when(is_last)
        def _():
            far_re, far_im = both_sides(fout[item, 0], fout[item, 1], far_table)
            residual = far_re * far_re + far_im * far_im - 0.25 * counts[item].astype(jnp.float32)
            back_re, back_im = both_sides(residual * far_re, -residual * far_im, far_table)
            bin_[item, 0] = back_re
            bin_[item, 1] = back_im

    def backward(item):
        @pl.when(jnp.logical_not(is_last))
        def _():
            backward_copy(item).wait_recv()

        real, imag = bin_[item, 0], bin_[item, 1]
        for layer in reversed(range(layers)):
            real, imag = both_sides(real, imag, prop_table)
            if layer > 0:
                wave_re, wave_im = mid[item, layer - 1, 0], mid[item, layer - 1, 1]
            else:
                wave_re, wave_im = fin[item, 0], fin[item, 1]
            delta[item, layer, 0] = wave_re * real - wave_im * imag
            delta[item, layer, 1] = -(wave_re * imag + wave_im * real)
            obj_re, obj_im = win[item, layer, 0], win[item, layer, 1]
            real, imag = real * obj_re - imag * obj_im, real * obj_im + imag * obj_re

        @pl.when(jnp.logical_not(is_first))
        def _():
            bout[item, 0] = real
            bout[item, 1] = imag
            backward_copy(item).start()

    lag = 2 * (depth_n - 1 - depth)

    @pl.loop(0, positions + 2 * (depth_n - 1))
    def _(step):
        @pl.when(step < positions)
        def _():
            forward(step)

        item = step - lag

        @pl.when((item >= 0) & (item < positions))
        def _():
            backward(item)

    @pl.when(jnp.logical_not(is_last))
    def _():
        @pl.loop(0, positions)
        def _(item):
            forward_copy(item).wait_send()

    @pl.when(jnp.logical_not(is_first))
    def _():
        @pl.loop(0, positions)
        def _(item):
            backward_copy(item).wait_send()


def call(body, shape, in_specs, scratch=(), collective=None):
    extra = {} if collective is None else {"collective_id": collective, "has_side_effects": True}
    return pl.pallas_call(
        body,
        out_shape=jax.ShapeDtypeStruct(shape, jnp.float32),
        in_specs=in_specs,
        out_specs=pl.BlockSpec(memory_space=pltpu.VMEM),
        scratch_shapes=list(scratch),
        compiler_params=pltpu.CompilerParams(vmem_limit_bytes=40 * 1024 * 1024, **extra),
    )


def shards(sizes, objects, probe_wave, offsets, counts):
    depth_n, dp_n, sub_n = sizes
    layers, _, half, width = objects.shape
    side = half * sub_n
    positions, size = counts.shape[0], counts.shape[1]
    rows = side // (dp_n * sub_n)
    prop_table, far_table = constants(size)
    vmem = pl.BlockSpec(memory_space=pltpu.VMEM)
    smem = pl.BlockSpec(memory_space=pltpu.SMEM)
    dma = pltpu.SemaphoreType.DMA

    def block(*shape):
        return pltpu.VMEM(shape, jnp.float32)

    full = call(
        functools.partial(gather_kernel, sub_n),
        (layers, 2, side, width),
        [vmem],
        [dma((sub_n,)), dma((sub_n,)), dma],
        0,
    )(objects)
    windows = (positions, layers, 2, size, size)
    win = call(window_kernel, windows, [smem, vmem])(offsets, full)
    waves = (positions, 2, size, size)
    delta = call(
        functools.partial(wave_kernel, depth_n),
        windows,
        [vmem] * 5,
        [
            block(*waves),
            block(positions, max(layers - 1, 1), 2, size, size),
            block(*waves),
            block(*waves),
            block(*waves),
        ]
        + [dma((positions,))] * 4,
        1,
    )(win, probe_wave, counts, jnp.asarray(prop_table), jnp.asarray(far_table))
    grad = call(scatter_kernel, (layers, 2, side + 8, width), [smem, vmem])(offsets, delta)
    return call(
        functools.partial(sum_kernel, dp_n, sub_n),
        (layers, 2, rows, width),
        [vmem],
        [
            block(layers, sub_n, dp_n, 2, rows, width),
            block(layers, dp_n, 2, rows, width),
            block(layers, dp_n, 2, rows, width),
            dma((layers, sub_n, dp_n)),
            dma((layers, sub_n, dp_n)),
            dma((layers, dp_n)),
            dma((layers, dp_n)),
        ],
        2,
    )(grad)


def solution(mesh):
    placed = (
        P(("groups", "depth"), None, "sub", None),
        P(),
        P(("groups", "dp", "sub"), None),
        P(("groups", "dp", "sub"), None, None),
    )
    sizes = tuple(mesh.shape[axis] for axis in ("depth", "dp", "sub"))
    return jax.shard_map(
        functools.partial(shards, sizes),
        mesh=mesh,
        in_specs=placed,
        out_specs=P(("groups", "depth"), None, ("dp", "sub"), None),
        check_vma=False,
    )
```

profile of v0, /device:TPU:0, one launch (start us, length us, event | category | flops | bytes accessed | tf_op | source)
XLA Modules:
  0.0 172.8 jit_solution(16718580382044423154)
XLA Ops:
  0.0 0.8 copy.8.offsets
  0.8 0.0 copy-start
  0.8 1.6 copy-done
  2.4 4.3 %shard_map.64.full = f32[2,2,512,512]{3,2,1,0:T(8,128)S(1)} custom-call(f32[2,2,256,512]{3,2,1,0:T(8,128)S(1)} %copy-done), custom_call_target="tpu_custom_call" | custom-call | tf_op jit(solution)/shard_map/pallas_call | solution.py:332
  6.6 0.0 copy-start.1
  6.7 0.0 copy-start.2
  6.7 0.0 copy-start.3
  6.7 0.0 copy-start.4
  6.7 3.4 %shard_map.65.win = f32[4,2,2,256,256]{4,3,2,1,0:T(8,128)S(1)} custom-call(s32[4,2]{1,0:T(4,128)S(1)} %copy.8.offsets, f32[2,2,512,512]{3,2,1,0:T(8,128)S(1)} %shard_map.64.full), custom_call_target="tpu_custom_call" | custom-call | tf_op jit(solution)/shard_map/pallas_call | solution.py:340
  10.1 0.0 copy-done.1
  10.1 0.0 copy-done.2
  10.1 0.0 copy-done.3
  10.1 0.0 copy-done.4
  10.1 130.2 %shard_map.66.delta = f32[4,2,2,256,256]{4,3,2,1,0:T(8,128)S(1)} custom-call(f32[4,2,2,256,256]{4,3,2,1,0:T(8,128)S(1)} %shard_map.65.win, f32[2,256,256]{2,1,0:T(8,128)S(1)} %copy-done.4, s32[4,256,256]{2,1,0:T(8,128)S(1)} %copy-done.3, bf16[4,512,512]{2,1,0:T(8,128)(2,1)S(1)} %copy-done.2, bf16[4,512,512]{2,1,0:T(8,128)(2,1)S(1)} %copy-done.1), custom_call_target="tpu_custom_call" | custom-call | tf_op jit(solution)/shard_map/pallas_call | solution.py:342
  140.3 3.0 %shard_map.67.grad = f32[2,2,520,512]{3,2,1,0:T(8,128)S(1)} custom-call(s32[4,2]{1,0:T(4,128)S(1)} %copy.8.offsets, f32[4,2,2,256,256]{4,3,2,1,0:T(8,128)S(1)} %shard_map.66.delta), custom_call_target="tpu_custom_call" | custom-call | tf_op jit(solution)/shard_map/pallas_call | solution.py:356
  143.3 28.4 %shard_map.68 = f32[2,2,128,512]{3,2,1,0:T(8,128)S(1)} custom-call(f32[2,2,520,512]{3,2,1,0:T(8,128)S(1)} %shard_map.67.grad), custom_call_target="tpu_custom_call" | custom-call | tf_op jit(solution)/shard_map/pallas_call | solution.py:357
  171.8 1.0 copy.10
Async XLA Ops:
  0.8 1.6 copy-start
  6.6 3.4 %copy-start.1 = (bf16[4,512,512]{2,1,0:T(8,128)(2,1)S(1)}, bf16[4,512,512]{2,1,0:T(8,128)(2,1)}, u32[]{:S(2)}) copy-start(bf16[4,512,512]{2,1,0:T(8,128)(2,1)} %constant.5.clone.far_table) | copy-start | bytes 6291460
  6.7 3.4 %copy-start.2 = (bf16[4,512,512]{2,1,0:T(8,128)(2,1)S(1)}, bf16[4,512,512]{2,1,0:T(8,128)(2,1)}, u32[]{:S(2)}) copy-start(bf16[4,512,512]{2,1,0:T(8,128)(2,1)} %constant.4.clone.prop_table) | copy-start | bytes 6291460
  6.7 3.4 %copy-start.3 = (s32[4,256,256]{2,1,0:T(8,128)S(1)}, s32[4,256,256]{2,1,0:T(8,128)}, u32[]{:S(2)}) copy-start(s32[4,256,256]{2,1,0:T(8,128)} %counts.1) | copy-start | bytes 3145732
  6.7 3.4 %copy-start.4 = (f32[2,256,256]{2,1,0:T(8,128)S(1)}, f32[2,256,256]{2,1,0:T(8,128)}, u32[]{:S(2)}) copy-start(f32[2,256,256]{2,1,0:T(8,128)} %probe.1) | copy-start | bytes 1572868
where the time goes:
time: 173 us
  Pallas kernels  169 us (98%)
  local copies, waits for them, and re-layouts  3.35 us (2%)
    pallas_call x1, Pallas kernels, shards(): call(functools.partial(wave_kernel, depth_n), windows, [vmem] * 5, [block...  130 us
    pallas_call x1, Pallas kernels, shards(): call(functools.partial(sum_kernel, dp_n, sub_n), (layers, 2, rows, width)...  28.4 us
    pallas_call x1, Pallas kernels, shards(): call(functools.partial(gather_kernel, sub_n), (layers, 2, side, width), [...  4.28 us

commit v1 on v0

--- a/solution.py
+++ b/solution.py
@@ -138,74 +138,72 @@
     dp, sub = lax.axis_index("dp"), lax.axis_index("sub")
     layers, _, rows, _ = out.shape
     greet(others("sub", sub_n) + others("dp", dp_n))
-    sub_copies = []
-    for layer in range(layers):
-        group = []
-        for shift in range(1, sub_n):
-            other = lax.rem(sub + shift, sub_n)
-            for chip in range(dp_n):
-                start = pl.multiple_of((chip * sub_n + other) * rows, rows)
-                copy = pltpu.make_async_remote_copy(
-                    src_ref=grad.at[layer, :, pl.ds(start, rows)],
-                    dst_ref=rsub.at[layer, shift, chip],
-                    send_sem=s_send.at[layer, shift, chip],
-                    recv_sem=s_recv.at[layer, shift, chip],
-                    device_id={"sub": other},
-                    device_id_type=MESH,
-                )
-                copy.start()
-                group.append(copy)
-        sub_copies.append(group)
-    dp_copies = []
-    for layer, group in enumerate(sub_copies):
-        for copy in group:
-            copy.wait()
-        for chip in range(dp_n):
-            start = pl.multiple_of((chip * sub_n + sub) * rows, rows)
-            total = grad[layer, :, pl.ds(start, rows), :]
+    pieces = [(layer, part) for layer in range(layers) for part in range(2)]
+
+    def sub_copy(layer, part, hop, shift):
+        other = lax.rem(sub + shift, sub_n)
+        chip = lax.rem(dp + hop, dp_n)
+        start = pl.multiple_of((chip * sub_n + other) * rows, rows)
+        return pltpu.make_async_remote_copy(
+            src_ref=grad.at[layer, part, pl.ds(start, rows)],
+            dst_ref=rsub.at[layer, part, hop, shift],
+            send_sem=s_send.at[layer, part, hop, shift],
+            recv_sem=s_recv.at[layer, part, hop, shift],
+            device_id={"sub": other},
+            device_id_type=MESH,
+        )
+
+    def dp_copy(layer, part, hop):
+        return pltpu.make_async_remote_copy(
+            src_ref=acc.at[layer, part, hop],
+            dst_ref=rdp.at[layer, part, hop],
+            send_sem=d_send.at[layer, part, hop],
+            recv_sem=d_recv.at[layer, part, hop],
+            device_id={"dp": lax.rem(dp + hop, dp_n)},
+            device_id_type=MESH,
+        )
+
+    hops = list(range(1, dp_n)) + [0]
+    for hop in hops:
+        for layer, part in pieces:
             for shift in range(1, sub_n):
-                total = total + rsub[layer, shift, chip]
-            acc[layer, chip] = total
-        group = []
-        for shift in range(1, dp_n):
-            other = lax.rem(dp + shift, dp_n)
-            copy = pltpu.make_async_remote_copy(
-                src_ref=acc.at[layer, other],
-                dst_ref=rdp.at[layer, shift],
-                send_sem=d_send.at[layer, shift],
-                recv_sem=d_recv.at[layer, shift],
-                device_id={"dp": other},
-                device_id_type=MESH,
-            )
-            copy.start()
-            group.append(copy)
-        dp_copies.append(group)
-    for layer, group in enumerate(dp_copies):
-        for copy in group:
-            copy.wait()
-        total = acc[layer, dp]
-        for shift in range(1, dp_n):
-            total = total + rdp[layer, shift]
-        out[layer] = total
+                sub_copy(layer, part, hop, shift).start()
+    for hop in hops:
+        chip = lax.rem(dp + hop, dp_n)
+        start = pl.multiple_of((chip * sub_n + sub) * rows, rows)
+        for layer, part in pieces:
+            total = grad[layer, part, pl.ds(start, rows), :]
+            for shift in range(1, sub_n):
+                sub_copy(layer, part, hop, shift).wait()
+                total = total + rsub[layer, part, hop, shift]
+            acc[layer, part, hop] = total
+            if hop > 0:
+                dp_copy(layer, part, hop).start()
+    for layer, part in pieces:
+        total = acc[layer, part, 0]
+        for hop in range(1, dp_n):
+            dp_copy(layer, part, hop).wait()
+            total = total + rdp[layer, part, hop]
+        out[layer, part] = total
 
 
 def wave_kernel(
-    depth_n, win, probe, counts, prop_table, far_table, delta,
-    fin, mid, fout, bin_, bout, f_send, f_recv, b_send, b_recv,
+    depth_n, sub_n, win, probe, counts, prop_table, far_table, delta,
+    fin, mid, fout, bin_, bout, f_send, f_recv, b_send, b_recv, turn,
 ):
-    depth = lax.axis_index("depth")
+    depth, sub = lax.axis_index("depth"), lax.axis_index("sub")
     positions, layers, _, size, _ = win.shape
     is_first, is_last = depth == 0, depth == depth_n - 1
     following = lax.rem(depth + 1, depth_n)
     previous = lax.rem(depth + depth_n - 1, depth_n)
-    greet([("depth", following), ("depth", previous)])
-
-    def forward_copy(item):
+    greet([("depth", following), ("depth", previous)] + others("sub", sub_n))
+
+    def forward_copy(item, part):
         return pltpu.make_async_remote_copy(
-            src_ref=fout.at[item],
-            dst_ref=fin.at[item],
-            send_sem=f_send.at[item],
-            recv_sem=f_recv.at[item],
+            src_ref=fout.at[item, part],
+            dst_ref=fin.at[item, part],
+            send_sem=f_send.at[item, part],
+            recv_sem=f_recv.at[item, part],
             device_id={"depth": following},
             device_id_type=MESH,
         )
@@ -227,7 +225,8 @@
 
         @pl.when(jnp.logical_not(is_first))
         def _():
-            forward_copy(item).wait_recv()
+            forward_copy(item, 0).wait_recv()
+            forward_copy(item, 1).wait_recv()
 
         real, imag = fin[item, 0], fin[item, 1]
         for layer in range(layers):
@@ -241,9 +240,24 @@
         fout[item, 0] = real
         fout[item, 1] = imag
 
+        @pl.when(is_first & ((sub > 0) | (item > 0)))
+        def _():
+            pl.semaphore_wait(turn, 1)
+
         @pl.when(jnp.logical_not(is_last))
         def _():
-            forward_copy(item).start()
+            forward_copy(item, 0).start()
+            forward_copy(item, 1).start()
+
+        @pl.when(is_first)
+        def _():
+            forward_copy(item, 0).wait_send()
+
+        @pl.when(is_first & ((sub < sub_n - 1) | (item < positions - 1)))
+        def _():
+            pl.semaphore_signal(
+                turn, inc=1, device_id={"sub": lax.rem(sub + 1, sub_n)}, device_id_type=MESH
+            )
 
         @pl.when(is_last)
         def _():
@@ -294,7 +308,11 @@
     def _():
         @pl.loop(0, positions)
         def _(item):
-            forward_copy(item).wait_send()
+            forward_copy(item, 1).wait_send()
+
+            @pl.when(jnp.logical_not(is_first))
+            def _():
+                forward_copy(item, 0).wait_send()
 
     @pl.when(jnp.logical_not(is_first))
     def _():
@@ -340,7 +358,7 @@
     win = call(window_kernel, windows, [smem, vmem])(offsets, full)
     waves = (positions, 2, size, size)
     delta = call(
-        functools.partial(wave_kernel, depth_n),
+        functools.partial(wave_kernel, depth_n, sub_n),
         windows,
         [vmem] * 5,
         [
@@ -350,7 +368,9 @@
             block(*waves),
             block(*waves),
         ]
-        + [dma((positions,))] * 4,
+        + [dma((positions, 2))] * 2
+        + [dma((positions,))] * 2
+        + [pltpu.SemaphoreType.REGULAR],
         1,
     )(win, probe_wave, counts, jnp.asarray(prop_table), jnp.asarray(far_table))
     grad = call(scatter_kernel, (layers, 2, side + 8, width), [smem, vmem])(offsets, delta)
@@ -359,13 +379,13 @@
         (layers, 2, rows, width),
         [vmem],
         [
-            block(layers, sub_n, dp_n, 2, rows, width),
-            block(layers, dp_n, 2, rows, width),
-            block(layers, dp_n, 2, rows, width),
-            dma((layers, sub_n, dp_n)),
-            dma((layers, sub_n, dp_n)),
-            dma((layers, dp_n)),
-            dma((layers, dp_n)),
+            block(layers, 2, dp_n, sub_n, rows, width),
+            block(layers, 2, dp_n, rows, width),
+            block(layers, 2, dp_n, rows, width),
+            dma((layers, 2, dp_n, sub_n)),
+            dma((layers, 2, dp_n, sub_n)),
+            dma((layers, 2, dp_n)),
+            dma((layers, 2, dp_n)),
         ],
         2,
     )(grad)

time: 173 us -> 178 us (1.029)
  Pallas kernels: 169 us -> 174 us
    pallas_call x1, Pallas kernels: 130 us -> 136 us  [shards(): call(functools.partial(wave_kernel, depth_n, sub_n), windows, [vmem] * 5,...]
where the time goes in v1:
time: 178 us; the launch traced here: 177 us
  Pallas kernels  174 us (98%)
  local copies, waits for them, and re-layouts  3.35 us (2%)
    pallas_call x1, Pallas kernels, shards(): call(functools.partial(wave_kernel, depth_n, sub_n), windows, [vmem] * 5,...  136 us
    pallas_call x1, Pallas kernels, shards(): call(functools.partial(sum_kernel, dp_n, sub_n), (layers, 2, rows, width)...  27.4 us
    pallas_call x1, Pallas kernels, shards(): call(functools.partial(gather_kernel, sub_n), (layers, 2, side, width), [...  4.28 us

profile of v1, /device:TPU:0, one launch (start us, length us, event | category | flops | bytes accessed | tf_op | source)
XLA Modules:
  0.0 177.4 jit_solution(2044369697820310598)
XLA Ops:
  0.0 0.8 copy.8.offsets
  0.8 0.0 copy-start
  0.8 1.6 copy-done
  2.4 4.3 %shard_map.64.full = f32[2,2,512,512]{3,2,1,0:T(8,128)S(1)} custom-call(f32[2,2,256,512]{3,2,1,0:T(8,128)S(1)} %copy-done), custom_call_target="tpu_custom_call" | custom-call | tf_op jit(solution)/shard_map/pallas_call | solution.py:350
  6.6 0.0 copy-start.1
  6.7 0.0 copy-start.2
  6.7 0.0 copy-start.3
  6.7 0.0 copy-start.4
  6.7 3.4 %shard_map.65.win = f32[4,2,2,256,256]{4,3,2,1,0:T(8,128)S(1)} custom-call(s32[4,2]{1,0:T(4,128)S(1)} %copy.8.offsets, f32[2,2,512,512]{3,2,1,0:T(8,128)S(1)} %shard_map.64.full), custom_call_target="tpu_custom_call" | custom-call | tf_op jit(solution)/shard_map/pallas_call | solution.py:358
  10.1 0.0 copy-done.1
  10.1 0.0 copy-done.2
  10.1 0.0 copy-done.3
  10.1 0.0 copy-done.4
  10.1 135.9 %shard_map.66.delta = f32[4,2,2,256,256]{4,3,2,1,0:T(8,128)S(1)} custom-call(f32[4,2,2,256,256]{4,3,2,1,0:T(8,128)S(1)} %shard_map.65.win, f32[2,256,256]{2,1,0:T(8,128)S(1)} %copy-done.4, s32[4,256,256]{2,1,0:T(8,128)S(1)} %copy-done.3, bf16[4,512,512]{2,1,0:T(8,128)(2,1)S(1)} %copy-done.2, bf16[4,512,512]{2,1,0:T(8,128)(2,1)S(1)} %copy-done.1), custom_call_target="tpu_custom_call" | custom-call | tf_op jit(solution)/shard_map/pallas_call | solution.py:360
  146.0 3.0 %shard_map.67.grad = f32[2,2,520,512]{3,2,1,0:T(8,128)S(1)} custom-call(s32[4,2]{1,0:T(4,128)S(1)} %copy.8.offsets, f32[4,2,2,256,256]{4,3,2,1,0:T(8,128)S(1)} %shard_map.66.delta), custom_call_target="tpu_custom_call" | custom-call | tf_op jit(solution)/shard_map/pallas_call | solution.py:376
  149.1 27.4 %shard_map.68 = f32[2,2,128,512]{3,2,1,0:T(8,128)S(1)} custom-call(f32[2,2,520,512]{3,2,1,0:T(8,128)S(1)} %shard_map.67.grad), custom_call_target="tpu_custom_call" | custom-call | tf_op jit(solution)/shard_map/pallas_call | solution.py:377
  176.5 1.0 copy.10
Async XLA Ops:
  0.8 1.6 copy-start
  6.6 3.4 %copy-start.1 = (bf16[4,512,512]{2,1,0:T(8,128)(2,1)S(1)}, bf16[4,512,512]{2,1,0:T(8,128)(2,1)}, u32[]{:S(2)}) copy-start(bf16[4,512,512]{2,1,0:T(8,128)(2,1)} %constant.5.clone.far_table) | copy-start | bytes 6291460
  6.7 3.4 %copy-start.2 = (bf16[4,512,512]{2,1,0:T(8,128)(2,1)S(1)}, bf16[4,512,512]{2,1,0:T(8,128)(2,1)}, u32[]{:S(2)}) copy-start(bf16[4,512,512]{2,1,0:T(8,128)(2,1)} %constant.4.clone.prop_table) | copy-start | bytes 6291460
  6.7 3.4 %copy-start.3 = (s32[4,256,256]{2,1,0:T(8,128)S(1)}, s32[4,256,256]{2,1,0:T(8,128)}, u32[]{:S(2)}) copy-start(s32[4,256,256]{2,1,0:T(8,128)} %counts.1) | copy-start | bytes 3145732
  6.7 3.4 %copy-start.4 = (f32[2,256,256]{2,1,0:T(8,128)S(1)}, f32[2,256,256]{2,1,0:T(8,128)}, u32[]{:S(2)}) copy-start(f32[2,256,256]{2,1,0:T(8,128)} %probe.1) | copy-start | bytes 1572868

commit v2 on v1

--- a/solution.py
+++ b/solution.py
@@ -188,22 +188,23 @@
 
 
 def wave_kernel(
-    depth_n, sub_n, win, probe, counts, prop_table, far_table, delta,
-    fin, mid, fout, bin_, bout, f_send, f_recv, b_send, b_recv, turn,
+    depth_n, win, probe, counts, tables, delta,
+    waves, fout, bin_, bout, state, f_send, f_recv, b_send, b_recv,
 ):
-    depth, sub = lax.axis_index("depth"), lax.axis_index("sub")
+    depth = lax.axis_index("depth")
     positions, layers, _, size, _ = win.shape
     is_first, is_last = depth == 0, depth == depth_n - 1
+    not_first, not_last = depth > 0, depth < depth_n - 1
     following = lax.rem(depth + 1, depth_n)
     previous = lax.rem(depth + depth_n - 1, depth_n)
-    greet([("depth", following), ("depth", previous)] + others("sub", sub_n))
-
-    def forward_copy(item, part):
+    greet([("depth", following), ("depth", previous)])
+
+    def forward_copy(item):
         return pltpu.make_async_remote_copy(
-            src_ref=fout.at[item, part],
-            dst_ref=fin.at[item, part],
-            send_sem=f_send.at[item, part],
-            recv_sem=f_recv.at[item, part],
+            src_ref=fout.at[item],
+            dst_ref=waves.at[item, 0],
+            send_sem=f_send.at[item],
+            recv_sem=f_recv.at[item],
             device_id={"depth": following},
             device_id_type=MESH,
         )
@@ -218,103 +219,95 @@
             device_id_type=MESH,
         )
 
-    def forward(item):
-        @pl.when(is_first)
-        def _():
-            fin[item] = probe[...]
-
-        @pl.when(jnp.logical_not(is_first))
-        def _():
-            forward_copy(item, 0).wait_recv()
-            forward_copy(item, 1).wait_recv()
-
-        real, imag = fin[item, 0], fin[item, 1]
-        for layer in range(layers):
-            if layer > 0:
-                mid[item, layer - 1, 0] = real
-                mid[item, layer - 1, 1] = imag
-            obj_re, obj_im = win[item, layer, 0], win[item, layer, 1]
-            real, imag = both_sides(
-                real * obj_re - imag * obj_im, real * obj_im + imag * obj_re, prop_table
-            )
-        fout[item, 0] = real
-        fout[item, 1] = imag
-
-        @pl.when(is_first & ((sub > 0) | (item > 0)))
-        def _():
-            pl.semaphore_wait(turn, 1)
-
-        @pl.when(jnp.logical_not(is_last))
-        def _():
-            forward_copy(item, 0).start()
-            forward_copy(item, 1).start()
-
-        @pl.when(is_first)
-        def _():
-            forward_copy(item, 0).wait_send()
-
-        @pl.when(is_first & ((sub < sub_n - 1) | (item < positions - 1)))
-        def _():
-            pl.semaphore_signal(
-                turn, inc=1, device_id={"sub": lax.rem(sub + 1, sub_n)}, device_id_type=MESH
-            )
-
-        @pl.when(is_last)
-        def _():
-            far_re, far_im = both_sides(fout[item, 0], fout[item, 1], far_table)
-            residual = far_re * far_re + far_im * far_im - 0.25 * counts[item].astype(jnp.float32)
-            back_re, back_im = both_sides(residual * far_re, -residual * far_im, far_table)
-            bin_[item, 0] = back_re
-            bin_[item, 1] = back_im
-
-    def backward(item):
-        @pl.when(jnp.logical_not(is_last))
-        def _():
-            backward_copy(item).wait_recv()
-
-        real, imag = bin_[item, 0], bin_[item, 1]
-        for layer in reversed(range(layers)):
-            real, imag = both_sides(real, imag, prop_table)
-            if layer > 0:
-                wave_re, wave_im = mid[item, layer - 1, 0], mid[item, layer - 1, 1]
-            else:
-                wave_re, wave_im = fin[item, 0], fin[item, 1]
-            delta[item, layer, 0] = wave_re * real - wave_im * imag
-            delta[item, layer, 1] = -(wave_re * imag + wave_im * real)
-            obj_re, obj_im = win[item, layer, 0], win[item, layer, 1]
-            real, imag = real * obj_re - imag * obj_im, real * obj_im + imag * obj_re
-
-        @pl.when(jnp.logical_not(is_first))
-        def _():
-            bout[item, 0] = real
-            bout[item, 1] = imag
-            backward_copy(item).start()
-
     lag = 2 * (depth_n - 1 - depth)
+    far, far_back, back = layers, layers + 1, layers + 2
 
     @pl.loop(0, positions + 2 * (depth_n - 1))
     def _(step):
-        @pl.when(step < positions)
-        def _():
-            forward(step)
-
-        item = step - lag
-
-        @pl.when((item >= 0) & (item < positions))
-        def _():
-            backward(item)
-
-    @pl.when(jnp.logical_not(is_last))
+        @pl.loop(0, 2 * layers + 2)
+        def _(phase):
+            is_back = phase >= back
+            item = jnp.where(is_back, step - lag, step)
+            is_far = (phase == far) | (phase == far_back)
+            active = (item >= 0) & (item < positions) & (jnp.logical_not(is_far) | is_last)
+
+            @pl.when(active)
+            def _():
+                @pl.when(phase == 0)
+                def _():
+                    @pl.when(is_first)
+                    def _():
+                        waves[item, 0] = probe[...]
+
+                    @pl.when(not_first)
+                    def _():
+                        forward_copy(item).wait_recv()
+
+                @pl.when((phase > 0) & (phase < layers))
+                def _():
+                    waves[item, phase] = state[...]
+
+                @pl.when(phase < layers)
+                def _():
+                    real, imag = waves[item, phase, 0], waves[item, phase, 1]
+                    obj_re, obj_im = win[item, phase, 0], win[item, phase, 1]
+                    state[0] = real * obj_re - imag * obj_im
+                    state[1] = real * obj_im + imag * obj_re
+
+                @pl.when(phase == back)
+                def _():
+                    @pl.when(not_last)
+                    def _():
+                        backward_copy(item).wait_recv()
+
+                    state[...] = bin_[item]
+
+                table = tables.at[jnp.where(is_far, 1, 0)]
+                real, imag = both_sides(state[0], state[1], table)
+                state[0] = real
+                state[1] = imag
+
+                @pl.when((phase == layers - 1) & not_last)
+                def _():
+                    fout[item] = state[...]
+                    forward_copy(item).start()
+
+                @pl.when(phase == far)
+                def _():
+                    far_re, far_im = state[0], state[1]
+                    residual = (
+                        far_re * far_re + far_im * far_im - 0.25 * counts[item].astype(jnp.float32)
+                    )
+                    state[0] = residual * far_re
+                    state[1] = -residual * far_im
+
+                @pl.when(phase == far_back)
+                def _():
+                    bin_[item] = state[...]
+
+                @pl.when(is_back)
+                def _():
+                    layer = 2 * layers + 1 - phase
+                    real, imag = state[0], state[1]
+                    wave_re, wave_im = waves[item, layer, 0], waves[item, layer, 1]
+                    delta[item, layer, 0] = wave_re * real - wave_im * imag
+                    delta[item, layer, 1] = -(wave_re * imag + wave_im * real)
+                    obj_re, obj_im = win[item, layer, 0], win[item, layer, 1]
+                    state[0] = real * obj_re - imag * obj_im
+                    state[1] = real * obj_im + imag * obj_re
+
+                    @pl.when((layer == 0) & not_first)
+                    def _():
+                        bout[item] = state[...]
+                        backward_copy(item).start()
+
+    @pl.when(not_last)
     def _():
         @pl.loop(0, positions)
         def _(item):
-            forward_copy(item, 1).wait_send()
-
-            @pl.when(jnp.logical_not(is_first))
-            def _():
-                forward_copy(item, 0).wait_send()
-
-    @pl.when(jnp.logical_not(is_first))
+            forward_copy(item).wait_send()
+
+    @pl.when(not_first)
     def _():
         @pl.loop(0, positions)
         def _(item):
@@ -358,21 +351,13 @@
     win = call(window_kernel, windows, [smem, vmem])(offsets, full)
     waves = (positions, 2, size, size)
     delta = call(
-        functools.partial(wave_kernel, depth_n, sub_n),
+        functools.partial(wave_kernel, depth_n),
         windows,
-        [vmem] * 5,
-        [
-            block(*waves),
-            block(positions, max(layers - 1, 1), 2, size, size),
-            block(*waves),
-            block(*waves),
-            block(*waves),
-        ]
-        + [dma((positions, 2))] * 2
-        + [dma((positions,))] * 2
-        + [pltpu.SemaphoreType.REGULAR],
+        [vmem] * 4,
+        [block(*windows), block(*waves), block(*waves), block(*waves), block(2, size, size)]
+        + [dma((positions,))] * 4,
         1,
-    )(win, probe_wave, counts, jnp.asarray(prop_table), jnp.asarray(far_table))
+    )(win, probe_wave, counts, jnp.asarray(np.stack([prop_table, far_table])))
     grad = call(scatter_kernel, (layers, 2, side + 8, width), [smem, vmem])(offsets, delta)
     return call(
         functools.partial(sum_kernel, dp_n, sub_n),

time: 178 us -> 171 us (0.961)
  Pallas kernels: 174 us -> 167 us
    pallas_call x1, Pallas kernels: 136 us -> 129 us  [shards(): call(functools.partial(wave_kernel, depth_n), windows, [vmem] * 4, [block...]
where the time goes in v2:
time: 171 us
  Pallas kernels  167 us (98%)
  local copies, waits for them, and re-layouts  3.35 us (2%)
    pallas_call x1, Pallas kernels, shards(): call(functools.partial(wave_kernel, depth_n), windows, [vmem] * 4, [block...  129 us
    pallas_call x1, Pallas kernels, shards(): call(functools.partial(sum_kernel, dp_n, sub_n), (layers, 2, rows, width)...  27.4 us
    pallas_call x1, Pallas kernels, shards(): call(functools.partial(gather_kernel, sub_n), (layers, 2, side, width), [...  4.28 us

profile of v2, /device:TPU:0, one launch (start us, length us, event | category | flops | bytes accessed | tf_op | source)
XLA Modules:
  0.0 170.7 jit_solution(9117622272915972867)
XLA Ops:
  0.0 0.8 copy.7.offsets
  0.8 0.0 copy-start.1
  0.8 1.6 copy-done.1
  2.4 4.3 %shard_map.55.full = f32[2,2,512,512]{3,2,1,0:T(8,128)S(1)} custom-call(f32[2,2,256,512]{3,2,1,0:T(8,128)S(1)} %copy-done.1), custom_call_target="tpu_custom_call" | custom-call | tf_op jit(solution)/shard_map/pallas_call | solution.py:343
  6.6 0.0 copy-start
  6.7 0.0 copy-start.2
  6.7 0.0 copy-start.3
  6.7 3.4 %shard_map.56.win = f32[4,2,2,256,256]{4,3,2,1,0:T(8,128)S(1)} custom-call(s32[4,2]{1,0:T(4,128)S(1)} %copy.7.offsets, f32[2,2,512,512]{3,2,1,0:T(8,128)S(1)} %shard_map.55.full), custom_call_target="tpu_custom_call" | custom-call | tf_op jit(solution)/shard_map/pallas_call | solution.py:351
  10.1 0.0 copy-done
  10.1 0.0 copy-done.2
  10.1 0.0 copy-done.3
  10.1 129.2 %shard_map.57.delta = f32[4,2,2,256,256]{4,3,2,1,0:T(8,128)S(1)} custom-call(f32[4,2,2,256,256]{4,3,2,1,0:T(8,128)S(1)} %shard_map.56.win, f32[2,256,256]{2,1,0:T(8,128)S(1)} %copy-done.3, s32[4,256,256]{2,1,0:T(8,128)S(1)} %copy-done.2, bf16[2,4,512,512]{3,2,1,0:T(8,128)(2,1)S(1)} %copy-done), custom_call_target="tpu_custom_call" | custom-call | tf_op jit(solution)/shard_map/pallas_call | solution.py:353
  139.3 3.0 %shard_map.58.grad = f32[2,2,520,512]{3,2,1,0:T(8,128)S(1)} custom-call(s32[4,2]{1,0:T(4,128)S(1)} %copy.7.offsets, f32[4,2,2,256,256]{4,3,2,1,0:T(8,128)S(1)} %shard_map.57.delta), custom_call_target="tpu_custom_call" | custom-call | tf_op jit(solution)/shard_map/pallas_call | solution.py:361
  142.3 27.4 %shard_map.59 = f32[2,2,128,512]{3,2,1,0:T(8,128)S(1)} custom-call(f32[2,2,520,512]{3,2,1,0:T(8,128)S(1)} %shard_map.58.grad), custom_call_target="tpu_custom_call" | custom-call | tf_op jit(solution)/shard_map/pallas_call | solution.py:362
  169.7 1.0 copy.9
Async XLA Ops:
  0.8 1.6 copy-start.1
  6.6 3.4 %copy-start = (bf16[2,4,512,512]{3,2,1,0:T(8,128)(2,1)S(1)}, bf16[2,4,512,512]{3,2,1,0:T(8,128)(2,1)}, u32[]{:S(2)}) copy-start(bf16[2,4,512,512]{3,2,1,0:T(8,128)(2,1)} %constant.2.clone.tables) | copy-start | bytes 12582916
  6.7 3.4 %copy-start.2 = (s32[4,256,256]{2,1,0:T(8,128)S(1)}, s32[4,256,256]{2,1,0:T(8,128)}, u32[]{:S(2)}) copy-start(s32[4,256,256]{2,1,0:T(8,128)} %counts.1) | copy-start | bytes 3145732
  6.7 3.4 %copy-start.3 = (f32[2,256,256]{2,1,0:T(8,128)S(1)}, f32[2,256,256]{2,1,0:T(8,128)}, u32[]{:S(2)}) copy-start(f32[2,256,256]{2,1,0:T(8,128)} %probe.1) | copy-start | bytes 1572868

commit v3 on v2

--- a/solution.py
+++ b/solution.py
@@ -188,8 +188,8 @@
 
 
 def wave_kernel(
-    depth_n, win, probe, counts, tables, delta,
-    waves, fout, bin_, bout, state, f_send, f_recv, b_send, b_recv,
+    depth_n, win, probe, counts, stored_tables, delta,
+    waves, fout, bin_, bout, state, tables, f_send, f_recv, b_send, b_recv, fetched,
 ):
     depth = lax.axis_index("depth")
     positions, layers, _, size, _ = win.shape
@@ -197,7 +197,10 @@
     not_first, not_last = depth > 0, depth < depth_n - 1
     following = lax.rem(depth + 1, depth_n)
     previous = lax.rem(depth + depth_n - 1, depth_n)
+    fetch = pltpu.make_async_copy(stored_tables, tables, fetched)
+    fetch.start()
     greet([("depth", following), ("depth", previous)])
+    fetch.wait()
 
     def forward_copy(item):
         return pltpu.make_async_remote_copy(
@@ -270,6 +273,11 @@
                 @pl.when((phase == layers - 1) & not_last)
                 def _():
                     fout[item] = state[...]
+
+                    @pl.when(is_first & (item > 0))
+                    def _():
+                        forward_copy(item - 1).wait_send()
+
                     forward_copy(item).start()
 
                 @pl.when(phase == far)
@@ -289,23 +297,30 @@
                 def _():
                     layer = 2 * layers + 1 - phase
                     real, imag = state[0], state[1]
+                    obj_re, obj_im = win[item, layer, 0], win[item, layer, 1]
+
+                    @pl.when(layer > 0)
+                    def _():
+                        state[0] = real * obj_re - imag * obj_im
+                        state[1] = real * obj_im + imag * obj_re
+
+                    @pl.when((layer == 0) & not_first)
+                    def _():
+                        bout[item, 0] = real * obj_re - imag * obj_im
+                        bout[item, 1] = real * obj_im + imag * obj_re
+                        backward_copy(item).start()
+
                     wave_re, wave_im = waves[item, layer, 0], waves[item, layer, 1]
                     delta[item, layer, 0] = wave_re * real - wave_im * imag
                     delta[item, layer, 1] = -(wave_re * imag + wave_im * real)
-                    obj_re, obj_im = win[item, layer, 0], win[item, layer, 1]
-                    state[0] = real * obj_re - imag * obj_im
-                    state[1] = real * obj_im + imag * obj_re
-
-                    @pl.when((layer == 0) & not_first)
-                    def _():
-                        bout[item] = state[...]
-                        backward_copy(item).start()
 
     @pl.when(not_last)
     def _():
         @pl.loop(0, positions)
         def _(item):
-            forward_copy(item).wait_send()
+            @pl.when(not_first | (item == positions - 1))
+            def _():
+                forward_copy(item).wait_send()
 
     @pl.when(not_first)
     def _():
@@ -332,7 +347,7 @@
     side = half * sub_n
     positions, size = counts.shape[0], counts.shape[1]
     rows = side // (dp_n * sub_n)
-    prop_table, far_table = constants(size)
+    tables = np.stack(constants(size))
     vmem = pl.BlockSpec(memory_space=pltpu.VMEM)
     smem = pl.BlockSpec(memory_space=pltpu.SMEM)
     dma = pltpu.SemaphoreType.DMA
@@ -353,11 +368,13 @@
     delta = call(
         functools.partial(wave_kernel, depth_n),
         windows,
-        [vmem] * 4,
+        [vmem] * 3 + [pl.BlockSpec(memory_space=pl.ANY)],
         [block(*windows), block(*waves), block(*waves), block(*waves), block(2, size, size)]
-        + [dma((positions,))] * 4,
+        + [pltpu.VMEM(tables.shape, tables.dtype)]
+        + [dma((positions,))] * 4
+        + [dma],
         1,
-    )(win, probe_wave, counts, jnp.asarray(np.stack([prop_table, far_table])))
+    )(win, probe_wave, counts, jnp.asarray(tables))
     grad = call(scatter_kernel, (layers, 2, side + 8, width), [smem, vmem])(offsets, delta)
     return call(
         functools.partial(sum_kernel, dp_n, sub_n),

time: 171 us -> 170 us (level)
  no operation moved by 1% of the time
where the time goes in v3:
time: 170 us
  Pallas kernels  167 us (98%)
  local copies, waits for them, and re-layouts  3.35 us (2%)
    pallas_call x1, Pallas kernels, shards(): call(functools.partial(wave_kernel, depth_n), windows, [vmem] * 3 + [pl.B...  129 us
    pallas_call x1, Pallas kernels, shards(): call(functools.partial(sum_kernel, dp_n, sub_n), (layers, 2, rows, width)...  27.4 us
    pallas_call x1, Pallas kernels, shards(): call(functools.partial(gather_kernel, sub_n), (layers, 2, side, width), [...  4.28 us

profile of v3, /device:TPU:0, one launch (start us, length us, event | category | flops | bytes accessed | tf_op | source)
XLA Modules:
  0.0 170.2 jit_solution(5184979475857738198)
XLA Ops:
  0.0 0.8 copy.7.offsets
  0.8 0.0 copy-start.1
  0.8 1.6 copy-done.1
  2.4 4.3 %shard_map.55.full = f32[2,2,512,512]{3,2,1,0:T(8,128)S(1)} custom-call(f32[2,2,256,512]{3,2,1,0:T(8,128)S(1)} %copy-done.1), custom_call_target="tpu_custom_call" | custom-call | tf_op jit(solution)/shard_map/pallas_call | solution.py:358
  6.6 0.0 copy-start
  6.7 0.0 copy-start.2
  6.7 0.0 copy-start.3
  6.7 3.4 %shard_map.56.win = f32[4,2,2,256,256]{4,3,2,1,0:T(8,128)S(1)} custom-call(s32[4,2]{1,0:T(4,128)S(1)} %copy.7.offsets, f32[2,2,512,512]{3,2,1,0:T(8,128)S(1)} %shard_map.55.full), custom_call_target="tpu_custom_call" | custom-call | tf_op jit(solution)/shard_map/pallas_call | solution.py:366
  10.1 0.0 copy-done
  10.1 0.0 copy-done.2
  10.1 0.0 copy-done.3
  10.1 128.7 %shard_map.57.delta = f32[4,2,2,256,256]{4,3,2,1,0:T(8,128)S(1)} custom-call(f32[4,2,2,256,256]{4,3,2,1,0:T(8,128)S(1)} %shard_map.56.win, f32[2,256,256]{2,1,0:T(8,128)S(1)} %copy-done.3, s32[4,256,256]{2,1,0:T(8,128)S(1)} %copy-done.2, bf16[2,4,512,512]{3,2,1,0:T(8,128)(2,1)S(1)} %copy-done), custom_call_target="tpu_custom_call" | custom-call | tf_op jit(solution)/shard_map/pallas_call | solution.py:368
  138.8 3.0 %shard_map.58.grad = f32[2,2,520,512]{3,2,1,0:T(8,128)S(1)} custom-call(s32[4,2]{1,0:T(4,128)S(1)} %copy.7.offsets, f32[4,2,2,256,256]{4,3,2,1,0:T(8,128)S(1)} %shard_map.57.delta), custom_call_target="tpu_custom_call" | custom-call | tf_op jit(solution)/shard_map/pallas_call | solution.py:378
  141.9 27.4 %shard_map.59 = f32[2,2,128,512]{3,2,1,0:T(8,128)S(1)} custom-call(f32[2,2,520,512]{3,2,1,0:T(8,128)S(1)} %shard_map.58.grad), custom_call_target="tpu_custom_call" | custom-call | tf_op jit(solution)/shard_map/pallas_call | solution.py:379
  169.3 1.0 copy.9
Async XLA Ops:
  0.8 1.6 copy-start.1
  6.6 3.4 %copy-start = (bf16[2,4,512,512]{3,2,1,0:T(8,128)(2,1)S(1)}, bf16[2,4,512,512]{3,2,1,0:T(8,128)(2,1)}, u32[]{:S(2)}) copy-start(bf16[2,4,512,512]{3,2,1,0:T(8,128)(2,1)} %constant.2.clone.stored_tables) | copy-start | bytes 12582916
  6.7 3.4 %copy-start.2 = (s32[4,256,256]{2,1,0:T(8,128)S(1)}, s32[4,256,256]{2,1,0:T(8,128)}, u32[]{:S(2)}) copy-start(s32[4,256,256]{2,1,0:T(8,128)} %counts.1) | copy-start | bytes 3145732
  6.7 3.4 %copy-start.3 = (f32[2,256,256]{2,1,0:T(8,128)S(1)}, f32[2,256,256]{2,1,0:T(8,128)}, u32[]{:S(2)}) copy-start(f32[2,256,256]{2,1,0:T(8,128)} %probe.1) | copy-start | bytes 1572868

commit v4 on v3

--- a/solution.py
+++ b/solution.py
@@ -223,16 +223,16 @@
         )
 
     lag = 2 * (depth_n - 1 - depth)
-    far, far_back, back = layers, layers + 1, layers + 2
+    far, back = layers - 1, layers
 
     @pl.loop(0, positions + 2 * (depth_n - 1))
     def _(step):
-        @pl.loop(0, 2 * layers + 2)
+        @pl.loop(0, 2 * layers)
         def _(phase):
             is_back = phase >= back
             item = jnp.where(is_back, step - lag, step)
-            is_far = (phase == far) | (phase == far_back)
-            active = (item >= 0) & (item < positions) & (jnp.logical_not(is_far) | is_last)
+            is_far = ((phase == far) | (phase == back)) & is_last
+            active = (item >= 0) & (item < positions)
 
             @pl.when(active)
             def _():
@@ -280,22 +280,18 @@
 
                     forward_copy(item).start()
 
-                @pl.when(phase == far)
+                @pl.when((phase == far) & is_last)
                 def _():
                     far_re, far_im = state[0], state[1]
                     residual = (
                         far_re * far_re + far_im * far_im - 0.25 * counts[item].astype(jnp.float32)
                     )
-                    state[0] = residual * far_re
-                    state[1] = -residual * far_im
-
-                @pl.when(phase == far_back)
-                def _():
-                    bin_[item] = state[...]
+                    bin_[item, 0] = residual * far_re
+                    bin_[item, 1] = -residual * far_im
 
                 @pl.when(is_back)
                 def _():
-                    layer = 2 * layers + 1 - phase
+                    layer = 2 * layers - 1 - phase
                     real, imag = state[0], state[1]
                     obj_re, obj_im = win[item, layer, 0], win[item, layer, 1]
 

time: 170 us -> 170 us (level)
  no operation moved by 1% of the time
where the time goes in v4:
time: 170 us; the launch traced here: 169 us
  Pallas kernels  166 us (98%)
  local copies, waits for them, and re-layouts  3.35 us (2%)
    pallas_call x1, Pallas kernels, shards(): call(functools.partial(wave_kernel, depth_n), windows, [vmem] * 3 + [pl.B...  128 us
    pallas_call x1, Pallas kernels, shards(): call(functools.partial(sum_kernel, dp_n, sub_n), (layers, 2, rows, width)...  27.4 us
    pallas_call x1, Pallas kernels, shards(): call(functools.partial(gather_kernel, sub_n), (layers, 2, side, width), [...  4.28 us

profile of v4, /device:TPU:0, one launch (start us, length us, event | category | flops | bytes accessed | tf_op | source)
XLA Modules:
  0.0 169.4 jit_solution(6498722383967965421)
XLA Ops:
  0.0 0.8 copy.7.offsets
  0.8 0.0 copy-start.1
  0.8 1.6 copy-done.1
  2.4 4.3 %shard_map.55.full = f32[2,2,512,512]{3,2,1,0:T(8,128)S(1)} custom-call(f32[2,2,256,512]{3,2,1,0:T(8,128)S(1)} %copy-done.1), custom_call_target="tpu_custom_call" | custom-call | tf_op jit(solution)/shard_map/pallas_call | solution.py:354
  6.6 0.0 copy-start
  6.7 0.0 copy-start.2
  6.7 0.0 copy-start.3
  6.7 3.4 %shard_map.56.win = f32[4,2,2,256,256]{4,3,2,1,0:T(8,128)S(1)} custom-call(s32[4,2]{1,0:T(4,128)S(1)} %copy.7.offsets, f32[2,2,512,512]{3,2,1,0:T(8,128)S(1)} %shard_map.55.full), custom_call_target="tpu_custom_call" | custom-call | tf_op jit(solution)/shard_map/pallas_call | solution.py:362
  10.1 0.0 copy-done
  10.1 0.0 copy-done.2
  10.1 0.0 copy-done.3
  10.1 127.9 %shard_map.57.delta = f32[4,2,2,256,256]{4,3,2,1,0:T(8,128)S(1)} custom-call(f32[4,2,2,256,256]{4,3,2,1,0:T(8,128)S(1)} %shard_map.56.win, f32[2,256,256]{2,1,0:T(8,128)S(1)} %copy-done.3, s32[4,256,256]{2,1,0:T(8,128)S(1)} %copy-done.2, bf16[2,4,512,512]{3,2,1,0:T(8,128)(2,1)S(1)} %copy-done), custom_call_target="tpu_custom_call" | custom-call | tf_op jit(solution)/shard_map/pallas_call | solution.py:364
  138.0 3.0 %shard_map.58.grad = f32[2,2,520,512]{3,2,1,0:T(8,128)S(1)} custom-call(s32[4,2]{1,0:T(4,128)S(1)} %copy.7.offsets, f32[4,2,2,256,256]{4,3,2,1,0:T(8,128)S(1)} %shard_map.57.delta), custom_call_target="tpu_custom_call" | custom-call | tf_op jit(solution)/shard_map/pallas_call | solution.py:374
  141.1 27.4 %shard_map.59 = f32[2,2,128,512]{3,2,1,0:T(8,128)S(1)} custom-call(f32[2,2,520,512]{3,2,1,0:T(8,128)S(1)} %shard_map.58.grad), custom_call_target="tpu_custom_call" | custom-call | tf_op jit(solution)/shard_map/pallas_call | solution.py:375
  168.5 1.0 copy.9
Async XLA Ops:
  0.8 1.6 copy-start.1
  6.6 3.4 %copy-start = (bf16[2,4,512,512]{3,2,1,0:T(8,128)(2,1)S(1)}, bf16[2,4,512,512]{3,2,1,0:T(8,128)(2,1)}, u32[]{:S(2)}) copy-start(bf16[2,4,512,512]{3,2,1,0:T(8,128)(2,1)} %constant.2.clone.stored_tables) | copy-start | bytes 12582916
  6.7 3.4 %copy-start.2 = (s32[4,256,256]{2,1,0:T(8,128)S(1)}, s32[4,256,256]{2,1,0:T(8,128)}, u32[]{:S(2)}) copy-start(s32[4,256,256]{2,1,0:T(8,128)} %counts.1) | copy-start | bytes 3145732
  6.7 3.4 %copy-start.3 = (f32[2,256,256]{2,1,0:T(8,128)S(1)}, f32[2,256,256]{2,1,0:T(8,128)}, u32[]{:S(2)}) copy-start(f32[2,256,256]{2,1,0:T(8,128)} %probe.1) | copy-start | bytes 1572868

commit v5 on v4

--- a/solution.py
+++ b/solution.py
@@ -188,7 +188,7 @@
 
 
 def wave_kernel(
-    depth_n, win, probe, counts, stored_tables, delta,
+    depth_n, win, probe, counts, prop_table, far_table, delta,
     waves, fout, bin_, bout, state, tables, f_send, f_recv, b_send, b_recv, fetched,
 ):
     depth = lax.axis_index("depth")
@@ -197,10 +197,15 @@
     not_first, not_last = depth > 0, depth < depth_n - 1
     following = lax.rem(depth + 1, depth_n)
     previous = lax.rem(depth + depth_n - 1, depth_n)
-    fetch = pltpu.make_async_copy(stored_tables, tables, fetched)
-    fetch.start()
+    fetches = [
+        pltpu.make_async_copy(table, tables.at[slot], fetched.at[slot])
+        for slot, table in enumerate((prop_table, far_table))
+    ]
+    for fetch in fetches:
+        fetch.start()
     greet([("depth", following), ("depth", previous)])
-    fetch.wait()
+    for fetch in fetches:
+        fetch.wait()
 
     def forward_copy(item):
         return pltpu.make_async_remote_copy(
@@ -364,13 +369,13 @@
     delta = call(
         functools.partial(wave_kernel, depth_n),
         windows,
-        [vmem] * 3 + [pl.BlockSpec(memory_space=pl.ANY)],
+        [vmem] * 3 + [pl.BlockSpec(memory_space=pl.ANY)] * 2,
         [block(*windows), block(*waves), block(*waves), block(*waves), block(2, size, size)]
         + [pltpu.VMEM(tables.shape, tables.dtype)]
         + [dma((positions,))] * 4
-        + [dma],
+        + [dma((2,))],
         1,
-    )(win, probe_wave, counts, jnp.asarray(tables))
+    )(win, probe_wave, counts, jnp.asarray(tables[0]), jnp.asarray(tables[1]))
     grad = call(scatter_kernel, (layers, 2, side + 8, width), [smem, vmem])(offsets, delta)
     return call(
         functools.partial(sum_kernel, dp_n, sub_n),

time: 170 us -> 170 us (level)
  no operation moved by 1% of the time
where the time goes in v5:
time: 170 us; the launch traced here: 169 us
  Pallas kernels  166 us (98%)
  local copies, waits for them, and re-layouts  3.35 us (2%)
    pallas_call x1, Pallas kernels, shards(): call(functools.partial(wave_kernel, depth_n), windows, [vmem] * 3 + [pl.B...  128 us
    pallas_call x1, Pallas kernels, shards(): call(functools.partial(sum_kernel, dp_n, sub_n), (layers, 2, rows, width)...  27.4 us
    pallas_call x1, Pallas kernels, shards(): call(functools.partial(gather_kernel, sub_n), (layers, 2, side, width), [...  4.28 us

profile of v5, /device:TPU:0, one launch (start us, length us, event | category | flops | bytes accessed | tf_op | source)
XLA Modules:
  0.0 169.5 jit_solution(6187745847435663281)
XLA Ops:
  0.0 0.8 copy.8.offsets
  0.8 0.0 copy-start
  0.8 1.6 copy-done
  2.4 4.3 %shard_map.64.full = f32[2,2,512,512]{3,2,1,0:T(8,128)S(1)} custom-call(f32[2,2,256,512]{3,2,1,0:T(8,128)S(1)} %copy-done), custom_call_target="tpu_custom_call" | custom-call | tf_op jit(solution)/shard_map/pallas_call | solution.py:359
  6.6 0.0 copy-start.1
  6.7 0.0 copy-start.2
  6.7 0.0 copy-start.3
  6.7 0.0 copy-start.4
  6.7 3.4 %shard_map.65.win = f32[4,2,2,256,256]{4,3,2,1,0:T(8,128)S(1)} custom-call(s32[4,2]{1,0:T(4,128)S(1)} %copy.8.offsets, f32[2,2,512,512]{3,2,1,0:T(8,128)S(1)} %shard_map.64.full), custom_call_target="tpu_custom_call" | custom-call | tf_op jit(solution)/shard_map/pallas_call | solution.py:367
  10.1 0.0 copy-done.1
  10.1 0.0 copy-done.2
  10.1 0.0 copy-done.3
  10.1 0.0 copy-done.4
  10.1 127.9 %shard_map.66.delta = f32[4,2,2,256,256]{4,3,2,1,0:T(8,128)S(1)} custom-call(f32[4,2,2,256,256]{4,3,2,1,0:T(8,128)S(1)} %shard_map.65.win, f32[2,256,256]{2,1,0:T(8,128)S(1)} %copy-done.4, s32[4,256,256]{2,1,0:T(8,128)S(1)} %copy-done.3, bf16[4,512,512]{2,1,0:T(8,128)(2,1)S(1)} %copy-done.2, bf16[4,512,512]{2,1,0:T(8,128)(2,1)S(1)} %copy-done.1), custom_call_target="tpu_custom_call" | custom-call | tf_op jit(solution)/shard_map/pallas_call | solution.py:369
  138.1 3.0 %shard_map.67.grad = f32[2,2,520,512]{3,2,1,0:T(8,128)S(1)} custom-call(s32[4,2]{1,0:T(4,128)S(1)} %copy.8.offsets, f32[4,2,2,256,256]{4,3,2,1,0:T(8,128)S(1)} %shard_map.66.delta), custom_call_target="tpu_custom_call" | custom-call | tf_op jit(solution)/shard_map/pallas_call | solution.py:379
  141.1 27.4 %shard_map.68 = f32[2,2,128,512]{3,2,1,0:T(8,128)S(1)} custom-call(f32[2,2,520,512]{3,2,1,0:T(8,128)S(1)} %shard_map.67.grad), custom_call_target="tpu_custom_call" | custom-call | tf_op jit(solution)/shard_map/pallas_call | solution.py:380
  168.5 1.0 copy.10
Async XLA Ops:
  0.8 1.6 copy-start
  6.6 3.4 %copy-start.1 = (bf16[4,512,512]{2,1,0:T(8,128)(2,1)S(1)}, bf16[4,512,512]{2,1,0:T(8,128)(2,1)}, u32[]{:S(2)}) copy-start(bf16[4,512,512]{2,1,0:T(8,128)(2,1)} %constant.5.clone.far_table) | copy-start | bytes 6291460
  6.7 3.4 %copy-start.2 = (bf16[4,512,512]{2,1,0:T(8,128)(2,1)S(1)}, bf16[4,512,512]{2,1,0:T(8,128)(2,1)}, u32[]{:S(2)}) copy-start(bf16[4,512,512]{2,1,0:T(8,128)(2,1)} %constant.4.clone.prop_table) | copy-start | bytes 6291460
  6.7 3.4 %copy-start.3 = (s32[4,256,256]{2,1,0:T(8,128)S(1)}, s32[4,256,256]{2,1,0:T(8,128)}, u32[]{:S(2)}) copy-start(s32[4,256,256]{2,1,0:T(8,128)} %counts.1) | copy-start | bytes 3145732
  6.7 3.4 %copy-start.4 = (f32[2,256,256]{2,1,0:T(8,128)S(1)}, f32[2,256,256]{2,1,0:T(8,128)}, u32[]{:S(2)}) copy-start(f32[2,256,256]{2,1,0:T(8,128)} %probe.1) | copy-start | bytes 1572868
